TPU v7x, 512 devices: a whole 4x8x8 slice. The times are simulated.
512 devices in a mesh: panel: 2 (over core), grp: 8 (over y_hi, x), col: 32 (over z, y_lo).
Axes of the slice: x: 4, y: 8 (y_hi: 2, y_lo: 4; y = y_hi * 4 + y_lo), z: 8, core: 2. Of those that a mesh axis runs over, the one named last changes fastest.
Arguments:
- field: float32 [2, 256, 64, 1536], P('panel', 'col', 'grp'), may hold values from -6 to 6
- vel_theta: bfloat16 [2, 256, 64, 1536], P('panel', 'col', 'grp'), may hold values from -1 to 1
- vel_phi: bfloat16 [2, 256, 64, 1536], P('panel', 'col', 'grp'), may hold values from -1 to 1
- strip_cell: int32 [2, 64, 2], P('panel', 'grp'), may hold values from 0 to 10750, as said below
- strip_dir: int32 [2, 64, 2], P('panel', 'grp'), may hold values from 0 to 1
- radial_inverse: float32 [256, 256], replicated, as said below
Outputs:
- advanced: float32 [2, 256, 64, 1536], P('panel', 'col', 'grp')
Inputs may be any that keep to these rules, and one draw needn't show every extreme that they name: Row part strip_cell // 1536 lies in 0 to 6; the longitude lies in 0 to 46 for slot 0 and in 1488 to 1534 for slot 1. `radial_inverse`: A dense matrix with a dominant diagonal.
All inputs are finite; a program needn't handle non-finite values.
Results may differ from a plain program's by a relative error of at most 0.0003.
Values may be sent and summed in bfloat16 or wider, within the bound.
A program may use at most 64 MiB of HBM per device.

v0:
```python
import jax
import jax.numpy as jnp
from jax import lax
from jax.sharding import PartitionSpec as P

NPH = 1536
STEPS = 2


KAPPA = 0.2


def from_partner(block, axis, bit):
    count = lax.axis_size(axis)
    route = []
    for low in range(count):
        high = low | 1 << bit
        if high != low and high < count:
            route += [(low, high), (high, low)]
    return lax.ppermute(block, axis, route)


def with_halo(block, sides, width):
    for axis, dim in sides:
        count = lax.axis_size(axis)
        forward = [(i, i + 1) for i in range(count - 1)]
        backward = [(target, source) for source, target in forward]
        low = lax.ppermute(
            lax.slice_in_dim(block, block.shape[dim] - width, None, axis=dim), axis, forward
        )
        high = lax.ppermute(lax.slice_in_dim(block, 0, width, axis=dim), axis, backward)
        block = jnp.concatenate([low, block, high], axis=dim)
    return block


def stencil(padded, vel_t, vel_p):
    center = padded[:, 1:-1, 1:-1]
    north = padded[:, 2:, 1:-1]
    south = padded[:, :-2, 1:-1]
    east = padded[:, 1:-1, 2:]
    west = padded[:, 1:-1, :-2]
    return (
        center
        + KAPPA * (north + south + east + west - 4.0 * center)
        - 0.5 * vel_t * (north - south)
        - 0.5 * vel_p * (east - west)
    )


def strips_of(slab, cells, dirs, east_shift):
    levels, rows, width = slab.shape
    row_first = jnp.clip(cells // NPH, 0, rows - 2)
    col_first = cells % NPH - jnp.array([0, east_shift], dtype=jnp.int32)
    col_first = jnp.clip(col_first, 0, width - 2)
    flat_first = row_first * width + col_first
    flat_second = flat_first + jnp.where(dirs == 1, width, 1)
    flat_slab = slab.reshape(levels, rows * width)
    values = 0.5 * (flat_slab[:, flat_first] + flat_slab[:, flat_second])
    return from_partner(values, "panel", 0)


def per_device(field, vel_theta, vel_phi, strip_cell, strip_dir, radial_inverse):
    state = field[0]
    vel_t = vel_theta[0]
    vel_p = vel_phi[0]
    cells = strip_cell[0]
    dirs = strip_dir[0]
    vel_tf = vel_t.astype(jnp.float32)
    vel_pf = vel_p.astype(jnp.float32)
    for step in range(STEPS):
        ghosts = strips_of(state, cells, dirs, 0)
        padded = with_halo(state, (("grp", 1),), 1)
        west_col = jnp.pad(ghosts[:, :, 0:1], ((0, 0), (1, 1), (0, 0)))
        east_col = jnp.pad(ghosts[:, :, 1:2], ((0, 0), (1, 1), (0, 0)))
        padded = jnp.concatenate([west_col, padded, east_col], axis=2)
        star = stencil(padded, vel_tf, vel_pf)
        block = lax.all_to_all(star, "col", split_axis=2, concat_axis=0, tiled=True)
        solved = jnp.dot(
            radial_inverse,
            block.reshape(block.shape[0], -1),
            precision=lax.Precision.HIGHEST,
            preferred_element_type=jnp.float32,
        )
        solved = solved.reshape(block.shape)
        state = lax.all_to_all(solved, "col", split_axis=0, concat_axis=2, tiled=True)
    return state[None]


def solution(mesh):
    placed = (
        P("panel", "col", "grp", None),
        P("panel", "col", "grp", None),
        P("panel", "col", "grp", None),
        P("panel", "grp", None),
        P("panel", "grp", None),
        P(),
    )
    return jax.shard_map(
        per_device,
        mesh=mesh,
        in_specs=placed,
        out_specs=P("panel", "col", "grp", None),
        check_vma=False,
    )
```

profile of v0, /device:TPU:56, one launch (start us, length us, event | category | flops | bytes accessed | tf_op | source)
XLA Modules:
  0.0 200.5 jit_solution(16470840874506058798)
XLA Ops:
  0.0 0.0 copy-start
  0.0 0.8 compare_select_fusion
  0.8 0.1 copy.45
  0.9 0.1 reshape.280
  1.0 4.9 %copy.44 = f32[1,8,8,1536]{1,3,2,0:T(8,128)} copy(f32[1,8,8,1536]{3,2,1,0:T(8,128)} %param.8) | data formatting | bytes 786432 | tf_op args[0]
  5.9 0.1 copy.46
  5.9 0.1 reshape.288
  6.0 3.3 %gather_fusion = f32[16,8]{1,0:T(8,128)S(1)} fusion(f32[8,12288]{0,1:T(8,128)} %bitcast.98, s32[1024]{0:T(1024)S(1)} %pad_clamp_fusion.1), kind=kCustom, calls=%fused_computation | custom fusion | bytes 1088 | tf_op jit(solution)/shard_map/gather | solution.py:58
  9.4 3.3 %gather_fusion.1 = f32[16,8]{1,0:T(8,128)S(1)} fusion(f32[8,12288]{0,1:T(8,128)} %bitcast.99, s32[1024]{0:T(1024)S(1)} %pad_clamp_fusion), kind=kCustom, calls=%fused_computation.1 | custom fusion | bytes 1088 | tf_op jit(solution)/shard_map/gather | solution.py:58
  12.7 1.9 collective-permute-start.2
  14.7 0.1 fusion.16
  14.8 6.9 %collective-permute-start = (f32[8,1,1536]{2,1,0:T(1,128)S(1)}, f32[8,1,1536]{2,1,0:T(1,128)S(1)}, u32[]{:S(2)}, u32[]{:S(2)}) collective-permute-start(f32[8,1,1536]{2,1,0:T(1,128)S(1)} %get-tuple-element.10), channel_id=1, source_target_pairs={{32,0},{64,32},{96,64},{128,96},{160,128},{192,160},{224,192},{33,... | collective-permute-start | bytes 147464 | tf_op jit(solution)/shard_map/ppermute | solution.py:31
  21.7 1.9 collective-permute-start.1
  23.6 0.0 collective-permute-done.2
  23.6 0.1 copy.59
  23.8 0.1 copy.60
  23.9 0.0 collective-permute-done
  23.9 9.8 %collective-permute-done.1 = f32[8,1,1536]{2,1,0:T(1,128)S(1)} collective-permute-done((f32[8,1,1536]{2,1,0:T(1,128)S(1)}, f32[8,1,1536]{2,1,0:T(1,128)S(1)}, u32[]{:S(2)}, u32[]{:S(2)}) %collective-permute-start.1) | collective-permute-done | bytes 49184 | tf_op jit(solution)/shard_map/ppermute | solution.py:28
  33.7 0.0 copy-done.2
  33.7 0.6 fusion.4
  34.3 3.9 %copy.49 = f32[8,8,1536]{1,0,2:T(8,128)} copy(f32[8,8,1536]{2,1,0:T(8,128)S(1)} %fusion.4) | data formatting | bytes 786432 | tf_op jit(solution)/shard_map/sub | solution.py:43
  38.2 5.5 %reshape.320 = f32[32,1,3072]{2,1,0:T(1,128)S(1)} reshape(f32[1536,8,8]{2,1,0:T(8,128)} %bitcast.92) | data formatting | bytes 786432
  43.7 27.1 %all_to_all.63 = f32[32,1,3072]{2,1,0:T(1,128)S(1)} all-to-all(f32[32,1,3072]{2,1,0:T(1,128)S(1)} %reshape.320), channel_id=1, replica_groups=mesh['panel'=2,'grp'=8,'col'=32] {'col'}, dimensions={0} | all-to-all | bytes 786432 | tf_op jit(solution)/shard_map/all_to_all | solution.py:77
  70.7 0.5 broadcast.503
  71.2 1.6 reduce
  72.8 5.1 %reshape.321 = f32[1536,8,8]{2,1,0:T(8,128)} reshape(f32[32,3072]{1,0:T(8,128)S(1)} %reduce) | data formatting | bytes 786432
  77.9 4.7 %copy.50 = f32[8,8,32,48]{3,1,0,2:T(8,128)S(1)} copy(f32[8,8,32,48]{1,0,3,2:T(8,128)} %bitcast.93) | data formatting | bytes 786432 | tf_op jit(solution)/shard_map/all_to_all | solution.py:77
  82.6 0.3 reshape.273
  82.9 0.8 fusion.19
  83.7 0.4 copy.51
  84.1 1.0 reshape.322
  85.1 19.0 %all_to_all.64 = f32[32,1,3072]{2,1,0:T(1,128)S(1)} all-to-all(f32[32,1,3072]{2,1,0:T(1,128)S(1)} %reshape.322), channel_id=1, replica_groups=mesh['panel'=2,'grp'=8,'col'=32] {'col'}, dimensions={0} | all-to-all | bytes 786432 | tf_op jit(solution)/shard_map/all_to_all | solution.py:85
  104.1 1.6 reduce.1
  105.7 0.5 reshape.323
  106.1 4.3 %copy.53 = f32[8,8,32,48]{0,3,2,1:T(8,128)} copy(f32[8,8,32,48]{3,1,0,2:T(8,128)S(1)} %bitcast.96) | data formatting | bytes 786432 | tf_op jit(solution)/shard_map/all_to_all | solution.py:85
  110.4 3.3 %gather_fusion.2 = f32[16,8]{1,0:T(8,128)S(1)} fusion(f32[8,12288]{0,1:T(8,128)} %bitcast.100, s32[1024]{0:T(1024)S(1)} %pad_clamp_fusion.1), kind=kCustom, calls=%fused_computation.2 | custom fusion | bytes 1088 | tf_op jit(solution)/shard_map/gather | solution.py:58
  113.8 3.3 %gather_fusion.3 = f32[16,8]{1,0:T(8,128)S(1)} fusion(f32[8,12288]{0,1:T(8,128)} %bitcast.101, s32[1024]{0:T(1024)S(1)} %pad_clamp_fusion), kind=kCustom, calls=%fused_computation.3 | custom fusion | bytes 1088 | tf_op jit(solution)/shard_map/gather | solution.py:58
  117.1 0.6 copy.52
  117.8 0.1 copy.54
  117.9 1.9 collective-permute-start.5
  119.8 0.7 all_to_all.52
  120.5 0.1 fusion.15
  120.5 1.9 collective-permute-start.3
  122.5 3.9 %collective-permute-start.4 = (f32[8,1,1536]{2,1,0:T(1,128)S(1)}, f32[8,1,1536]{2,1,0:T(1,128)S(1)}, u32[]{:S(2)}, u32[]{:S(2)}) collective-permute-start(f32[8,1,1536]{2,1,0:T(1,128)S(1)} %get-tuple-element.7), channel_id=1, source_target_pairs={{0,32},{32,64},{64,96},{96,128},{128,160},{160,192},{192,224},{1,3... | collective-permute-start | bytes 147464 | tf_op jit(solution)/shard_map/ppermute | solution.py:28
  126.4 0.0 collective-permute-done.5
  126.4 0.1 fusion.17
  126.5 0.1 collective-permute-done.3
  126.6 7.9 %collective-permute-done.4 = f32[8,1,1536]{2,1,0:T(1,128)S(1)} collective-permute-done((f32[8,1,1536]{2,1,0:T(1,128)S(1)}, f32[8,1,1536]{2,1,0:T(1,128)S(1)}, u32[]{:S(2)}, u32[]{:S(2)}) %collective-permute-start.4) | collective-permute-done | bytes 49184 | tf_op jit(solution)/shard_map/ppermute | solution.py:28
  134.5 0.6 fusion.5
  135.1 3.9 %copy.55 = f32[8,8,1536]{1,0,2:T(8,128)} copy(f32[8,8,1536]{2,1,0:T(8,128)S(1)} %fusion.5) | data formatting | bytes 786432 | tf_op jit(solution)/shard_map/sub | solution.py:43
  139.0 5.5 %reshape.324 = f32[32,1,3072]{2,1,0:T(1,128)S(1)} reshape(f32[1536,8,8]{2,1,0:T(8,128)} %bitcast.94) | data formatting | bytes 786432
  144.5 19.1 %all_to_all.65 = f32[32,1,3072]{2,1,0:T(1,128)S(1)} all-to-all(f32[32,1,3072]{2,1,0:T(1,128)S(1)} %reshape.324), channel_id=1, replica_groups=mesh['panel'=2,'grp'=8,'col'=32] {'col'}, dimensions={0} | all-to-all | bytes 786432 | tf_op jit(solution)/shard_map/all_to_all | solution.py:77
  163.6 1.6 reduce.2
  165.2 5.1 %reshape.325 = f32[1536,8,8]{2,1,0:T(8,128)} reshape(f32[32,3072]{1,0:T(8,128)S(1)} %reduce.2) | data formatting | bytes 786432
  170.3 4.7 %copy.56 = f32[8,8,32,48]{3,1,0,2:T(8,128)S(1)} copy(f32[8,8,32,48]{1,0,3,2:T(8,128)} %bitcast.95) | data formatting | bytes 786432 | tf_op jit(solution)/shard_map/all_to_all | solution.py:77
  175.0 0.3 reshape.276
  175.3 0.8 fusion.20
  176.1 0.4 copy.57
  176.5 1.0 reshape.326
  177.5 19.0 %all_to_all.66 = f32[32,1,3072]{2,1,0:T(1,128)S(1)} all-to-all(f32[32,1,3072]{2,1,0:T(1,128)S(1)} %reshape.326), channel_id=1, replica_groups=mesh['panel'=2,'grp'=8,'col'=32] {'col'}, dimensions={0} | all-to-all | bytes 786432 | tf_op jit(solution)/shard_map/all_to_all | solution.py:85
  196.5 1.6 reduce.3
  198.0 0.5 reshape.327
  198.5 0.6 copy.58
  199.1 1.4 broadcast_in_dim.8
  (12 shorter events, 0.1 us)
Async XLA Ops:
  0.0 82.9 %copy-start = (f32[256,256]{1,0:T(8,128)S(1)}, f32[256,256]{1,0:T(8,128)}, u32[]{:S(2)}) copy-start(f32[256,256]{1,0:T(8,128)} %param.13) | copy-start | bytes 786436
  0.0 14.7 %copy-start.1 = (f32[1,8,8,1536]{3,2,1,0:T(8,128)S(1)}, f32[1,8,8,1536]{3,2,1,0:T(8,128)}, u32[]{:S(2)}) copy-start(f32[1,8,8,1536]{3,2,1,0:T(8,128)} %param.8) | copy-start | bytes 1179652
  0.0 33.7 %copy-start.2 = (bf16[1,8,8,1536]{3,2,1,0:T(8,128)(2,1)S(1)}, bf16[1,8,8,1536]{3,2,1,0:T(8,128)(2,1)}, u32[]{:S(2)}) copy-start(bf16[1,8,8,1536]{3,2,1,0:T(8,128)(2,1)} %param.10) | copy-start | bytes 589828
  0.0 33.7 %copy-start.3 = (bf16[1,8,8,1536]{3,2,1,0:T(8,128)(2,1)S(1)}, bf16[1,8,8,1536]{3,2,1,0:T(8,128)(2,1)}, u32[]{:S(2)}) copy-start(bf16[1,8,8,1536]{3,2,1,0:T(8,128)(2,1)} %param.9) | copy-start | bytes 589828
  12.7 10.9 %collective-permute-start.2 = (f32[8,8,2]{0,2,1:T(2,128)S(1)}, f32[8,8,2]{0,2,1:T(2,128)S(1)}, u32[]{:S(2)}, u32[]{:S(2)}) collective-permute-start(f32[8,8,2]{0,2,1:T(2,128)S(1)} %bitcast.111), channel_id=1, source_target_pairs={{0,256},{256,0},{1,257},{257,1},{2,258},{258,2},{3,259},{259,3},{4... | collective-permute-start | bytes 1544 | tf_op jit(solution)/shard_map/ppermute | solution.py:20
  14.8 9.1 %collective-permute-start = (f32[8,1,1536]{2,1,0:T(1,128)S(1)}, f32[8,1,1536]{2,1,0:T(1,128)S(1)}, u32[]{:S(2)}, u32[]{:S(2)}) collective-permute-start(f32[8,1,1536]{2,1,0:T(1,128)S(1)} %get-tuple-element.10), channel_id=1, source_target_pairs={{32,0},{64,32},{96,64},{128,96},{160,128},{192,160},{224,192},{33,... | collective-permute-start | bytes 147464 | tf_op jit(solution)/shard_map/ppermute | solution.py:31
  21.7 12.0 %collective-permute-start.1 = (f32[8,1,1536]{2,1,0:T(1,128)S(1)}, f32[8,1,1536]{2,1,0:T(1,128)S(1)}, u32[]{:S(2)}, u32[]{:S(2)}) collective-permute-start(f32[8,1,1536]{2,1,0:T(1,128)S(1)} %get-tuple-element.9), channel_id=1, source_target_pairs={{0,32},{32,64},{64,96},{96,128},{128,160},{160,192},{192,224},{1,3... | collective-permute-start | bytes 147464 | tf_op jit(solution)/shard_map/ppermute | solution.py:28
  117.9 8.5 %collective-permute-start.5 = (f32[8,8,2]{2,1,0:T(8,128)S(1)}, f32[8,8,2]{2,1,0:T(8,128)S(1)}, u32[]{:S(2)}, u32[]{:S(2)}) collective-permute-start(f32[8,8,2]{2,1,0:T(8,128)S(1)} %bitcast.110), channel_id=1, source_target_pairs={{0,256},{256,0},{1,257},{257,1},{2,258},{258,2},{3,259},{259,3},{4... | collective-permute-start | bytes 1544 | tf_op jit(solution)/shard_map/ppermute | solution.py:20
  120.5 6.0 %collective-permute-start.3 = (f32[8,1,1536]{2,1,0:T(1,128)S(1)}, f32[8,1,1536]{2,1,0:T(1,128)S(1)}, u32[]{:S(2)}, u32[]{:S(2)}) collective-permute-start(f32[8,1,1536]{2,1,0:T(1,128)S(1)} %get-tuple-element.8), channel_id=1, source_target_pairs={{32,0},{64,32},{96,64},{128,96},{160,128},{192,160},{224,192},{33,... | collective-permute-start | bytes 147464 | tf_op jit(solution)/shard_map/ppermute | solution.py:31
  122.5 12.1 %collective-permute-start.4 = (f32[8,1,1536]{2,1,0:T(1,128)S(1)}, f32[8,1,1536]{2,1,0:T(1,128)S(1)}, u32[]{:S(2)}, u32[]{:S(2)}) collective-permute-start(f32[8,1,1536]{2,1,0:T(1,128)S(1)} %get-tuple-element.7), channel_id=1, source_target_pairs={{0,32},{32,64},{64,96},{96,128},{128,160},{160,192},{192,224},{1,3... | collective-permute-start | bytes 147464 | tf_op jit(solution)/shard_map/ppermute | solution.py:28
where the time goes:
time: 201 us
  blocking collectives  84.1 us (42%)
  local copies, waits for them, and re-layouts  69.9 us (35%)
  starting transfers between devices  18.5 us (9%)
  waiting for transfers between devices  17.8 us (9%)
  other arithmetic  8.26 us (4%)
    all_to_all x2, blocking collectives, per_device(): block = lax.all_to_all(star, 'col', split_axis=2, concat_axis=0, tiled=True)  46.2 us
    all_to_all x2, blocking collectives, per_device(): lax.all_to_all(solved, 'col', split_axis=0, concat_axis=2, tiled=True)  37.9 us
    unnamed x19, local copies, waits for them, and re-layouts  29.1 us
    ppermute x2, waiting for transfers between devices, with_halo(): lax.ppermute(lax.slice_in_dim(block, block.shape[dim] - width, None, axis...  17.7 us
    gather x4, local copies, waits for them, and re-layouts, strips_of(): values = 0.5 * (flat_slab[:, flat_first] + flat_slab[:, flat_second])  13.4 us
    all_to_all x3, local copies, waits for them, and re-layouts, per_device(): block = lax.all_to_all(star, 'col', split_axis=2, concat_axis=0, tiled=True)  9.83 us
    ppermute x2, starting transfers between devices, with_halo(): lax.ppermute(lax.slice_in_dim(block, 0, width, axis=dim), axis, backward)  8.83 us
    sub x2, local copies, waits for them, and re-layouts, stencil(): center + KAPPA * (north + south + east + west - 4.0 * center)  7.83 us
  transfers between devices with their start and end apart: 6, of which 3 were waited for; matrix products, arithmetic and copies ran while one was open for 0% of the time, Pallas kernels for 0%

commit v1 on v0

v1 whole, which is shorter than its diff:
```python
import functools

import jax
import jax.numpy as jnp
from jax import lax
from jax.experimental import pallas as pl
from jax.experimental.pallas import tpu as pltpu
from jax.sharding import PartitionSpec as P

MESH = pl.DeviceIdType.MESH
KAPPA = 0.2
COLS = 32
LEV = 8
ROWS = 8
NPH = 1536
PHD = 48
NR = 256
CELLS = ROWS * PHD
GROUPS = NPH // CELLS
TILES = NPH // 128
VEL_ONE = 32767.0
F32 = jnp.float32
I32 = jnp.int32
BF16 = jnp.bfloat16


def to_int(x):
    return (x + jnp.where(x >= 0.0, 0.5, -0.5)).astype(I32)


def pack_vel(vt, vp):
    qt = to_int(vt.astype(F32) * VEL_ONE)
    qp = to_int(vp.astype(F32) * VEL_ONE)
    return (qt & 0xFFFF) | (qp << 16)


def half_vel(word):
    scale = 0.5 / VEL_ONE
    return ((word << 16) >> 16).astype(F32) * scale, (word >> 16).astype(F32) * scale


def swap_chunks(rows):
    lane = lax.broadcasted_iota(I32, rows[0].shape, 1)
    chunk = (lane * 1366) >> 16
    rows = list(rows)
    for bit in (1, 2, 4):
        inside = (chunk & bit) != 0
        for low in range(8):
            if low & bit:
                continue
            a, b = rows[low], rows[low | bit]
            rows[low] = jnp.where(inside, pltpu.roll(b, PHD * bit, 1), a)
            rows[low | bit] = jnp.where(inside, b, pltpu.roll(a, CELLS - PHD * bit, 1))
    return rows


def encode(x0, x1, x2):
    top = jnp.maximum(jnp.maximum(jnp.abs(x0), jnp.abs(x1)), jnp.abs(x2))
    top = jnp.max(top, axis=1, keepdims=True)
    top = jnp.broadcast_to(jnp.maximum(top, 1e-30), x0.shape)
    k = jnp.ceil(jnp.log2(top) * 4.0).astype(I32) + (1 - 4 * 17)
    inverse = jnp.exp2(k.astype(F32) * -0.25)
    q0, q1, q2 = (to_int(x * inverse) for x in (x0, x1, x2))
    return (
        (q0 << 14) | ((q1 >> 4) & 0x3FFF),
        (q2 << 14) | ((q1 & 15) << 10) | (k & 0x3FF),
    )


def decode(w0, w1):
    scale = jnp.exp2(((w1 << 22) >> 22).astype(F32) * 0.25)
    q1 = (((w0 << 18) >> 18) << 4) | ((w1 >> 10) & 15)
    return (
        (w0 >> 14).astype(F32) * scale,
        q1.astype(F32) * scale,
        (w1 >> 14).astype(F32) * scale,
    )


def halves(x):
    high = x.astype(BF16)
    return high, (x - high.astype(F32)).astype(BF16)


def dot3(a, b, dims):
    ah, al = a
    bh, bl = b
    mul = functools.partial(lax.dot_general, dimension_numbers=(dims, ((), ())), preferred_element_type=F32)
    return mul(ah, bh) + (mul(ah, bl) + mul(al, bh))


def kernel(
    cell_ref, dir_ref, field_hbm, vt_hbm, vp_hbm, mat_hbm,
    out_ref,
    field, vt, vp, mat, mat_h, mat_l, tmat_h, tmat_l,
    state, row_in, words, star, ghost_out, ghost_in,
    vel_out, vel_in, pack_out, pack_in, back_out, back_in,
    column, side_in, edge_out, edge_in, vel_col, star_col, solved, tiles,
    load_sem, send_sem, row_sem, ghost_sem, vela_sem, velb_sem, pack_sem, back_sem, side_sem, edge_sem,
):
    p = lax.axis_index("panel")
    g = lax.axis_index("grp")
    me = lax.axis_index("col")

    for k in range(TILES):
        pltpu.make_async_copy(field_hbm.at[:, pl.ds(128 * k, 128)], field.at[k], load_sem.at[0]).start()
    loads = [
        pltpu.make_async_copy(src, dst, load_sem.at[i])
        for i, (src, dst) in enumerate(((field, field), (vt_hbm, vt), (vp_hbm, vp), (mat_hbm, mat)))
    ]
    for copy in loads[1:]:
        copy.start()

    barrier = pltpu.get_barrier_semaphore()

    def greet(s, carry):
        pl.semaphore_signal(barrier, inc=1, device_id={"col": lax.rem(me + s, COLS)}, device_id_type=MESH)
        return carry

    lax.fori_loop(1, COLS, greet, 0)
    pl.semaphore_signal(barrier, inc=1, device_id={"panel": 1 - p}, device_id_type=MESH)

    @pl.when(g > 0)
    def _():
        pl.semaphore_signal(barrier, inc=1, device_id={"grp": g - 1}, device_id_type=MESH)

    @pl.when(g < 7)
    def _():
        pl.semaphore_signal(barrier, inc=1, device_id={"grp": g + 1}, device_id_type=MESH)

    loads[0].wait()
    for t in range(ROWS):
        for k in range(TILES):
            lanes = pl.ds(128 * k, 128)
            state[t, :, lanes] = field[k, pl.ds(t, LEV, stride=ROWS), :]

    @pl.when(g == 0)
    def _():
        row_in[0] = jnp.zeros((LEV, NPH), F32)

    @pl.when(g == 7)
    def _():
        row_in[1] = jnp.zeros((LEV, NPH), F32)

    lane = lax.broadcasted_iota(I32, (LEV, 128), 1)
    ghosts = jnp.zeros((LEV, 128), F32)
    for t in range(ROWS):
        for s in range(2):
            cell = cell_ref[s, t]
            d = dir_ref[s, t]
            r = lax.div(cell, NPH)
            c = cell - r * NPH - s * (NPH - 128)
            lanes = pl.ds(s * (NPH - 128), 128)
            first = state[r, :, lanes]
            second = state[r + d, :, lanes]
            both = jnp.where(lane == c, first, 0.0) + jnp.where(lane == c + 1 - d, second, 0.0)
            value = 0.5 * jnp.sum(both, axis=1, keepdims=True)
            ghosts = jnp.where(lane == 2 * t + s, value, ghosts)
    ghost_out[...] = ghosts

    loads[1].wait()
    loads[2].wait()
    for k in range(TILES):
        words[k] = pack_vel(vt[:, 128 * k : 128 * (k + 1)], vp[:, 128 * k : 128 * (k + 1)])

    def vel_group(q, carry):
        rows = []
        for t in range(ROWS):
            parts = [words[q * 3 + k, pl.ds(t, LEV, stride=ROWS), :] for k in range(3)]
            rows.append(jnp.concatenate(parts, axis=1))
        for d, row in enumerate(swap_chunks(rows)):
            vel_out[q * 8 + d] = row
        return carry

    lax.fori_loop(0, GROUPS, vel_group, 0)

    count = COLS + jnp.where(g > 0, 1, 0) + jnp.where(g < 7, 1, 0)
    pl.semaphore_wait(barrier, count)

    def row_copy(src, sem, target):
        return pltpu.make_async_remote_copy(
            src_ref=state.at[src], dst_ref=row_in.at[sem], send_sem=send_sem.at[sem], recv_sem=row_sem.at[sem],
            device_id={"grp": target}, device_id_type=MESH)

    up = row_copy(ROWS - 1, 0, g + 1)
    down = row_copy(0, 1, g - 1)

    @pl.when(g < 7)
    def _():
        up.start()

    @pl.when(g > 0)
    def _():
        down.start()

    ghost_copy = pltpu.make_async_remote_copy(
        src_ref=ghost_out, dst_ref=ghost_in, send_sem=send_sem.at[2], recv_sem=ghost_sem,
        device_id={"panel": 1 - p}, device_id_type=MESH)
    ghost_copy.start()

    def scatter(src, dst, lanes, send, recv):
        def part(ref, i):
            return ref.at[i] if lanes is None else ref.at[i, :, lanes]

        def one(s, carry):
            d = lax.rem(me + s, COLS)
            pltpu.make_async_remote_copy(
                src_ref=part(src, d), dst_ref=part(dst, me), send_sem=send, recv_sem=recv,
                device_id={"col": d}, device_id_type=MESH).start()
            return carry

        lax.fori_loop(1, COLS, one, 0)
        pltpu.make_async_copy(part(src, me), part(dst, me), recv).start()

    def arrived(dst, lanes, recv):
        whole = dst if lanes is None else dst.at[:, :, lanes]
        pltpu.make_async_copy(whole, whole, recv).wait()

    def sent(src, lanes, send):
        most = src.at[pl.ds(0, COLS - 1)] if lanes is None else src.at[pl.ds(0, COLS - 1), :, lanes]
        pltpu.make_async_copy(most, most, send).wait()

    first_part, second_part = pl.ds(0, 256), pl.ds(256, 128)
    scatter(vel_out, vel_in, first_part, send_sem.at[3], vela_sem)

    ghost_copy.wait_recv()

    @pl.when(g > 0)
    def _():
        up.wait_recv()

    @pl.when(g < 7)
    def _():
        down.wait_recv()

    wide = lax.broadcasted_iota(I32, (LEV, NPH), 1)
    ghosts = ghost_in[...]
    for t in range(ROWS):
        center = state[t]
        south = state[t - 1] if t > 0 else row_in[0]
        north = state[t + 1] if t < ROWS - 1 else row_in[1]
        west = jnp.where(wide == 0, ghosts[:, 2 * t : 2 * t + 1], pltpu.roll(center, 1, 1))
        east = jnp.where(wide == NPH - 1, ghosts[:, 2 * t + 1 : 2 * t + 2], pltpu.roll(center, NPH - 1, 1))
        word = jnp.concatenate(
            [words[k, pl.ds(t, LEV, stride=ROWS), :] for k in range(TILES)], axis=1)
        half_t, half_p = half_vel(word)
        star[t] = (
            center + KAPPA * (north + south + east + west - 4.0 * center)
            - half_t * (north - south) - half_p * (east - west)
        )

    def star_group(q, carry):
        lanes = pl.ds(pl.multiple_of(q * CELLS, 128), CELLS)
        rows = swap_chunks([star[t, :, lanes] for t in range(ROWS)])
        for d, row in enumerate(rows):
            w0, w1 = encode(row[:, 0:128], row[:, 128:256], row[:, 256:384])
            pack_out[q * 8 + d, :, 0:128] = w0
            pack_out[q * 8 + d, :, 128:256] = w1
        return carry

    lax.fori_loop(0, GROUPS, star_group, 0)
    scatter(pack_out, pack_in, None, send_sem.at[4], pack_sem)
    scatter(vel_out, vel_in, second_part, send_sem.at[5], velb_sem)

    loads[3].wait()
    matrix = mat[...]
    mat_h[...], mat_l[...] = halves(matrix)
    tmat_h[...], tmat_l[...] = halves(jnp.transpose(matrix))

    arrived(pack_in, None, pack_sem)
    w0 = pack_in[:, :, 0:128].reshape(NR, 128)
    w1 = pack_in[:, :, 128:256].reshape(NR, 128)
    for i, tile in enumerate(decode(w0, w1)):
        star_col[pl.ds(128 * i, 128), :] = jnp.transpose(tile)
    first = dot3(halves(star_col[...]), (tmat_h[...], tmat_l[...]), ((1,), (0,)))
    for t in range(ROWS):
        column[t, pl.ds(8, PHD), :] = first[t * PHD : (t + 1) * PHD]

    @pl.when(g == 0)
    def _():
        side_in[0] = jnp.zeros((PHD, NR), F32)

    @pl.when(g == 7)
    def _():
        side_in[1] = jnp.zeros((PHD, NR), F32)

    inner = pl.ds(8, PHD)

    def side_copy(src, sem, target):
        return pltpu.make_async_remote_copy(
            src_ref=column.at[src, inner], dst_ref=side_in.at[sem], send_sem=send_sem.at[sem + 6],
            recv_sem=side_sem.at[sem], device_id={"grp": target}, device_id_type=MESH)

    up2 = side_copy(ROWS - 1, 0, g + 1)
    down2 = side_copy(0, 1, g - 1)

    @pl.when(g < 7)
    def _():
        up2.start()

    @pl.when(g > 0)
    def _():
        down2.start()

    for s in range(2):
        at_end = me == s * (COLS - 1)
        for t in range(ROWS):
            cell = cell_ref[s, t]
            d = dir_ref[s, t]
            r = lax.div(cell, NPH)
            c = jnp.clip(cell - r * NPH - s * (NPH - PHD), 0, PHD - 2)
            own = s * (PHD - 1)
            row1 = jnp.where(at_end, r, t)
            row2 = jnp.where(at_end, r + d, t)
            col1 = jnp.where(at_end, c, own)
            col2 = jnp.where(at_end, c + 1 - d, own)
            edge_out[s, pl.ds(t, 1), :] = 0.5 * (
                column[row1, pl.ds(col1 + 8, 1), :] + column[row2, pl.ds(col2 + 8, 1), :])
    edge_copies = []
    for s in range(2):
        at_end = me == s * (COLS - 1)
        there = jnp.where(at_end, me, me + 2 * s - 1)
        panel = jnp.where(at_end, 1 - p, p)
        slot = jnp.where(at_end, s, 1 - s)
        copy = pltpu.make_async_remote_copy(
            src_ref=edge_out.at[s], dst_ref=edge_in.at[slot], send_sem=send_sem.at[8 + s], recv_sem=edge_sem.at[slot],
            device_id={"panel": panel, "col": there}, device_id_type=MESH)
        copy.start()
        edge_copies.append(copy)

    arrived(vel_in, first_part, vela_sem)
    arrived(vel_in, second_part, velb_sem)
    for i in range(3):
        vel_col[pl.ds(128 * i, 128), :] = jnp.transpose(vel_in[:, :, 128 * i : 128 * (i + 1)].reshape(NR, 128))

    for s in range(2):
        pltpu.make_async_copy(edge_in.at[s], edge_in.at[s], edge_sem.at[s]).wait()
    for t in range(ROWS):
        column[t, pl.ds(7, 1), :] = edge_in[0, pl.ds(t, 1), :]
        column[t, pl.ds(8 + PHD, 1), :] = edge_in[1, pl.ds(t, 1), :]

    @pl.when(g > 0)
    def _():
        up2.wait_recv()

    @pl.when(g < 7)
    def _():
        down2.wait_recv()

    for t in range(ROWS):
        center = column[t, inner, :]
        south = column[t - 1, inner, :] if t > 0 else side_in[0]
        north = column[t + 1, inner, :] if t < ROWS - 1 else side_in[1]
        east = column[t, pl.ds(9, PHD), :]
        west = column[t, pl.ds(7, PHD), :]
        half_t, half_p = half_vel(vel_col[pl.ds(t * PHD, PHD), :])
        star_col[pl.ds(t * PHD, PHD), :] = (
            center + KAPPA * (north + south + east + west - 4.0 * center)
            - half_t * (north - south) - half_p * (east - west)
        )
    solved[...] = dot3((mat_h[...], mat_l[...]), halves(star_col[...]), ((1,), (1,)))

    def back_one(i, carry):
        rows = pl.ds(pl.multiple_of(i * LEV, LEV), LEV)
        w0, w1 = encode(solved[rows, 0:128], solved[rows, 128:256], solved[rows, 256:384])
        back_out[i, :, 0:128] = w0
        back_out[i, :, 128:256] = w1
        return carry

    lax.fori_loop(0, COLS, back_one, 0)
    scatter(back_out, back_in, None, send_sem.at[10], back_sem)

    @pl.when(g < 7)
    def _():
        up.wait_send()
        up2.wait_send()

    @pl.when(g > 0)
    def _():
        down.wait_send()
        down2.wait_send()

    ghost_copy.wait_send()
    for copy in edge_copies:
        copy.wait_send()
    sent(vel_out, first_part, send_sem.at[3])
    sent(pack_out, None, send_sem.at[4])
    sent(vel_out, second_part, send_sem.at[5])

    arrived(back_in, None, back_sem)

    def out_group(q, carry):
        rows = []
        for d in range(8):
            rows.append(jnp.concatenate(decode(back_in[q * 8 + d, :, 0:128], back_in[q * 8 + d, :, 128:256]), axis=1))
        for t, row in enumerate(swap_chunks(rows)):
            for k in range(3):
                tiles[q * 3 + k, pl.ds(t, LEV, stride=ROWS), :] = row[:, 128 * k : 128 * (k + 1)]
        for k in range(3):
            lanes = pl.ds(pl.multiple_of(q * CELLS + 128 * k, 128), 128)
            pltpu.make_async_copy(tiles.at[q * 3 + k], out_ref.at[:, lanes], load_sem.at[4]).start()
        return carry

    lax.fori_loop(0, GROUPS, out_group, 0)
    pltpu.make_async_copy(tiles, tiles, load_sem.at[4]).wait()
    sent(back_out, None, send_sem.at[10])


def per_device(field, vel_theta, vel_phi, strip_cell, strip_dir, radial_inverse):
    smem = pl.BlockSpec(memory_space=pltpu.SMEM)
    hbm = pl.BlockSpec(memory_space=pl.ANY)
    flat = (LEV * ROWS, NPH)
    tiled = (TILES, LEV * ROWS, 128)
    dma = pltpu.SemaphoreType.DMA
    out = pl.pallas_call(
        kernel,
        out_shape=jax.ShapeDtypeStruct(flat, F32),
        in_specs=[smem, smem, hbm, hbm, hbm, hbm],
        out_specs=pl.BlockSpec(memory_space=pltpu.VMEM),
        scratch_shapes=[
            pltpu.VMEM(tiled, F32), pltpu.VMEM(flat, BF16), pltpu.VMEM(flat, BF16), pltpu.VMEM((NR, NR), F32),
            pltpu.VMEM((NR, NR), BF16), pltpu.VMEM((NR, NR), BF16), pltpu.VMEM((NR, NR), BF16), pltpu.VMEM((NR, NR), BF16),
            pltpu.VMEM((ROWS, LEV, NPH), F32), pltpu.VMEM((2, LEV, NPH), F32), pltpu.VMEM(tiled, I32), pltpu.VMEM((ROWS, LEV, NPH), F32),
            pltpu.VMEM((LEV, 128), F32), pltpu.VMEM((LEV, 128), F32),
            pltpu.VMEM((COLS, LEV, CELLS), I32), pltpu.VMEM((COLS, LEV, CELLS), I32),
            pltpu.VMEM((COLS, LEV, 256), I32), pltpu.VMEM((COLS, LEV, 256), I32),
            pltpu.VMEM((COLS, LEV, 256), I32), pltpu.VMEM((COLS, LEV, 256), I32),
            pltpu.VMEM((ROWS, 64, NR), F32), pltpu.VMEM((2, PHD, NR), F32),
            pltpu.VMEM((2, ROWS, NR), F32), pltpu.VMEM((2, ROWS, NR), F32),
            pltpu.VMEM((CELLS, NR), I32), pltpu.VMEM((CELLS, NR), F32), pltpu.VMEM((NR, CELLS), F32), pltpu.VMEM(tiled, F32),
            dma((5,)), dma((11,)), dma((2,)), dma, dma, dma, dma, dma, dma((2,)), dma((2,)),
        ],
        compiler_params=pltpu.CompilerParams(
            collective_id=0, has_side_effects=True, vmem_limit_bytes=60 * 2**20),
    )(
        strip_cell[0].T, strip_dir[0].T, field.reshape(flat), vel_theta.reshape(flat), vel_phi.reshape(flat),
        radial_inverse,
    )
    return out.reshape(1, LEV, ROWS, NPH)


def solution(mesh):
    placed = (
        P("panel", "col", "grp", None),
        P("panel", "col", "grp", None),
        P("panel", "col", "grp", None),
        P("panel", "grp", None),
        P("panel", "grp", None),
        P(),
    )
    return jax.shard_map(
        per_device, mesh=mesh, in_specs=placed, out_specs=P("panel", "col", "grp", None), check_vma=False)
```

time: 201 us -> 55.5 us (0.28)
  the two profiles are of different devices: /device:TPU:56 before, /device:TPU:6 now
where the time goes in v1:
time: 55.5 us; the launch traced here: 55.4 us
  Pallas kernels  53.6 us (97%)
  local copies, waits for them, and re-layouts  1.77 us (3%)
    pallas_call x1, Pallas kernels, per_device(): pl.pallas_call(kernel, out_shape=jax.ShapeDtypeStruct(flat, F32), in_spec...  53.6 us
    unnamed x1, local copies, waits for them, and re-layouts  1.77 us

profile of v1, /device:TPU:6, one launch (start us, length us, event | category | flops | bytes accessed | tf_op | source)
XLA Modules:
  0.0 55.4 jit_solution(2768395020557345251)
XLA Ops:
  0.0 53.6 %shard_map.64 = f32[64,1536]{1,0:T(8,128)} custom-call(s32[2,8]{1,0:T(2,128)} %bitcast.14, s32[2,8]{1,0:T(2,128)} %bitcast.15, f32[64,1536]{1,0:T(8,128)} %bitcast.11, bf16[64,1536]{1,0:T(8,128)(2,1)} %bitcast.12, bf16[64,1536]{1,0:T(8,128)(2,1)} %bitcast.13, f32[256,256]{1,0:T(8,128)} %mat_hbm.1), custom_call_target="tpu_custom_call" | custom-call | tf_op jit(solution)/shard_map/pallas_call | solution.py:415
  53.6 1.8 %copy.8 = f32[1,8,8,1536]{3,2,1,0:T(8,128)} copy(f32[1,8,8,1536]{3,2,1,0:T(8,128)} %bitcast.10) | data formatting | bytes 786432

commit v2 on v1

--- a/solution.py
+++ b/solution.py
@@ -54,9 +54,9 @@
     return rows
 
 
-def encode(x0, x1, x2):
+def encode(x0, x1, x2, axis=1):
     top = jnp.maximum(jnp.maximum(jnp.abs(x0), jnp.abs(x1)), jnp.abs(x2))
-    top = jnp.max(top, axis=1, keepdims=True)
+    top = jnp.max(top, axis=axis, keepdims=True)
     top = jnp.broadcast_to(jnp.maximum(top, 1e-30), x0.shape)
     k = jnp.ceil(jnp.log2(top) * 4.0).astype(I32) + (1 - 4 * 17)
     inverse = jnp.exp2(k.astype(F32) * -0.25)
@@ -93,9 +93,9 @@
     cell_ref, dir_ref, field_hbm, vt_hbm, vp_hbm, mat_hbm,
     out_ref,
     field, vt, vp, mat, mat_h, mat_l, tmat_h, tmat_l,
-    state, row_in, words, star, ghost_out, ghost_in,
+    state, row_out, row_in, halo, words, star, ghost_out, ghost_in,
     vel_out, vel_in, pack_out, pack_in, back_out, back_in,
-    column, side_in, edge_out, edge_in, vel_col, star_col, solved, tiles,
+    column, side_out, side_in, side, edge_out, edge_in, vel_col, star_col, solved, tiles,
     load_sem, send_sem, row_sem, ghost_sem, vela_sem, velb_sem, pack_sem, back_sem, side_sem, edge_sem,
 ):
     p = lax.axis_index("panel")
@@ -136,11 +136,17 @@
 
     @pl.when(g == 0)
     def _():
-        row_in[0] = jnp.zeros((LEV, NPH), F32)
+        halo[0] = jnp.zeros((LEV, NPH), F32)
 
     @pl.when(g == 7)
     def _():
-        row_in[1] = jnp.zeros((LEV, NPH), F32)
+        halo[1] = jnp.zeros((LEV, NPH), F32)
+
+    for i, t in enumerate((ROWS - 1, 0)):
+        for q in range(GROUPS):
+            w0, w1 = encode(*(state[t, :, CELLS * q + 128 * k : CELLS * q + 128 * (k + 1)] for k in range(3)))
+            row_out[i, :, 256 * q : 256 * q + 128] = w0
+            row_out[i, :, 256 * q + 128 : 256 * (q + 1)] = w1
 
     lane = lax.broadcasted_iota(I32, (LEV, 128), 1)
     ghosts = jnp.zeros((LEV, 128), F32)
@@ -177,13 +183,13 @@
     count = COLS + jnp.where(g > 0, 1, 0) + jnp.where(g < 7, 1, 0)
     pl.semaphore_wait(barrier, count)
 
-    def row_copy(src, sem, target):
+    def row_copy(sem, target):
         return pltpu.make_async_remote_copy(
-            src_ref=state.at[src], dst_ref=row_in.at[sem], send_sem=send_sem.at[sem], recv_sem=row_sem.at[sem],
+            src_ref=row_out.at[sem], dst_ref=row_in.at[sem], send_sem=send_sem.at[sem], recv_sem=row_sem.at[sem],
             device_id={"grp": target}, device_id_type=MESH)
 
-    up = row_copy(ROWS - 1, 0, g + 1)
-    down = row_copy(0, 1, g - 1)
+    up = row_copy(0, g + 1)
+    down = row_copy(1, g - 1)
 
     @pl.when(g < 7)
     def _():
@@ -212,6 +218,22 @@
         lax.fori_loop(1, COLS, one, 0)
         pltpu.make_async_copy(part(src, me), part(dst, me), recv).start()
 
+    def scatter_group(src, dst, q, send, recv):
+        for j in range(8):
+            d = q * 8 + j
+
+            @pl.when(d != me)
+            def _():
+                pltpu.make_async_remote_copy(
+                    src_ref=src.at[d], dst_ref=dst.at[me], send_sem=send, recv_sem=recv,
+                    device_id={"col": d}, device_id_type=MESH).start()
+
+            @pl.when(d == me)
+            def _():
+                pltpu.make_async_copy(src.at[d], dst.at[d], recv).start()
+
+    own_group = lax.div(me, 8)
+
     def arrived(dst, lanes, recv):
         whole = dst if lanes is None else dst.at[:, :, lanes]
         pltpu.make_async_copy(whole, whole, recv).wait()
@@ -220,25 +242,33 @@
         most = src.at[pl.ds(0, COLS - 1)] if lanes is None else src.at[pl.ds(0, COLS - 1), :, lanes]
         pltpu.make_async_copy(most, most, send).wait()
 
-    first_part, second_part = pl.ds(0, 256), pl.ds(256, 128)
+    first_part, second_part = pl.ds(0, 128), pl.ds(128, 256)
     scatter(vel_out, vel_in, first_part, send_sem.at[3], vela_sem)
 
     ghost_copy.wait_recv()
 
+    def unpack_row(i):
+        for q in range(GROUPS):
+            parts = decode(row_in[i, :, 256 * q : 256 * q + 128], row_in[i, :, 256 * q + 128 : 256 * (q + 1)])
+            for k, part in enumerate(parts):
+                halo[i, :, CELLS * q + 128 * k : CELLS * q + 128 * (k + 1)] = part
+
     @pl.when(g > 0)
     def _():
         up.wait_recv()
+        unpack_row(0)
 
     @pl.when(g < 7)
     def _():
         down.wait_recv()
+        unpack_row(1)
 
     wide = lax.broadcasted_iota(I32, (LEV, NPH), 1)
     ghosts = ghost_in[...]
     for t in range(ROWS):
         center = state[t]
-        south = state[t - 1] if t > 0 else row_in[0]
-        north = state[t + 1] if t < ROWS - 1 else row_in[1]
+        south = state[t - 1] if t > 0 else halo[0]
+        north = state[t + 1] if t < ROWS - 1 else halo[1]
         west = jnp.where(wide == 0, ghosts[:, 2 * t : 2 * t + 1], pltpu.roll(center, 1, 1))
         east = jnp.where(wide == NPH - 1, ghosts[:, 2 * t + 1 : 2 * t + 2], pltpu.roll(center, NPH - 1, 1))
         word = jnp.concatenate(
@@ -249,17 +279,18 @@
             - half_t * (north - south) - half_p * (east - west)
         )
 
-    def star_group(q, carry):
+    def star_group(i, carry):
+        q = lax.rem(own_group + i, GROUPS)
         lanes = pl.ds(pl.multiple_of(q * CELLS, 128), CELLS)
         rows = swap_chunks([star[t, :, lanes] for t in range(ROWS)])
         for d, row in enumerate(rows):
             w0, w1 = encode(row[:, 0:128], row[:, 128:256], row[:, 256:384])
             pack_out[q * 8 + d, :, 0:128] = w0
             pack_out[q * 8 + d, :, 128:256] = w1
+        scatter_group(pack_out, pack_in, q, send_sem.at[4], pack_sem)
         return carry
 
     lax.fori_loop(0, GROUPS, star_group, 0)
-    scatter(pack_out, pack_in, None, send_sem.at[4], pack_sem)
     scatter(vel_out, vel_in, second_part, send_sem.at[5], velb_sem)
 
     loads[3].wait()
@@ -278,21 +309,25 @@
 
     @pl.when(g == 0)
     def _():
-        side_in[0] = jnp.zeros((PHD, NR), F32)
+        side[0] = jnp.zeros((PHD, NR), F32)
 
     @pl.when(g == 7)
     def _():
-        side_in[1] = jnp.zeros((PHD, NR), F32)
+        side[1] = jnp.zeros((PHD, NR), F32)
 
     inner = pl.ds(8, PHD)
-
-    def side_copy(src, sem, target):
+    for i, t in enumerate((ROWS - 1, 0)):
+        w0, w1 = encode(*(column[t, 8 + 16 * k : 24 + 16 * k, :] for k in range(3)), axis=0)
+        side_out[i, 0:16, :] = w0
+        side_out[i, 16:32, :] = w1
+
+    def side_copy(sem, target):
         return pltpu.make_async_remote_copy(
-            src_ref=column.at[src, inner], dst_ref=side_in.at[sem], send_sem=send_sem.at[sem + 6],
+            src_ref=side_out.at[sem], dst_ref=side_in.at[sem], send_sem=send_sem.at[sem + 6],
             recv_sem=side_sem.at[sem], device_id={"grp": target}, device_id_type=MESH)
 
-    up2 = side_copy(ROWS - 1, 0, g + 1)
-    down2 = side_copy(0, 1, g - 1)
+    up2 = side_copy(0, g + 1)
+    down2 = side_copy(1, g - 1)
 
     @pl.when(g < 7)
     def _():
@@ -328,6 +363,10 @@
         copy.start()
         edge_copies.append(copy)
 
+    def unpack_side(i):
+        for k, part in enumerate(decode(side_in[i, 0:16, :], side_in[i, 16:32, :])):
+            side[i, 16 * k : 16 * (k + 1), :] = part
+
     arrived(vel_in, first_part, vela_sem)
     arrived(vel_in, second_part, velb_sem)
     for i in range(3):
@@ -342,15 +381,17 @@
     @pl.when(g > 0)
     def _():
         up2.wait_recv()
+        unpack_side(0)
 
     @pl.when(g < 7)
     def _():
         down2.wait_recv()
+        unpack_side(1)
 
     for t in range(ROWS):
         center = column[t, inner, :]
-        south = column[t - 1, inner, :] if t > 0 else side_in[0]
-        north = column[t + 1, inner, :] if t < ROWS - 1 else side_in[1]
+        south = column[t - 1, inner, :] if t > 0 else side[0]
+        north = column[t + 1, inner, :] if t < ROWS - 1 else side[1]
         east = column[t, pl.ds(9, PHD), :]
         west = column[t, pl.ds(7, PHD), :]
         half_t, half_p = half_vel(vel_col[pl.ds(t * PHD, PHD), :])
@@ -360,15 +401,16 @@
         )
     solved[...] = dot3((mat_h[...], mat_l[...]), halves(star_col[...]), ((1,), (1,)))
 
-    def back_one(i, carry):
-        rows = pl.ds(pl.multiple_of(i * LEV, LEV), LEV)
+    def back_group(i, carry):
+        q = lax.rem(own_group + i, GROUPS)
+        rows = pl.ds(pl.multiple_of(q * 64, 64), 64)
         w0, w1 = encode(solved[rows, 0:128], solved[rows, 128:256], solved[rows, 256:384])
-        back_out[i, :, 0:128] = w0
-        back_out[i, :, 128:256] = w1
+        back_out[pl.ds(q * 8, 8), :, 0:128] = w0.reshape(8, LEV, 128)
+        back_out[pl.ds(q * 8, 8), :, 128:256] = w1.reshape(8, LEV, 128)
+        scatter_group(back_out, back_in, q, send_sem.at[10], back_sem.at[own_group])
         return carry
 
-    lax.fori_loop(0, COLS, back_one, 0)
-    scatter(back_out, back_in, None, send_sem.at[10], back_sem)
+    lax.fori_loop(0, GROUPS, back_group, 0)
 
     @pl.when(g < 7)
     def _():
@@ -387,9 +429,10 @@
     sent(pack_out, None, send_sem.at[4])
     sent(vel_out, second_part, send_sem.at[5])
 
-    arrived(back_in, None, back_sem)
-
-    def out_group(q, carry):
+    def out_group(i, carry):
+        q = lax.rem(own_group + GROUPS - i, GROUPS)
+        part = back_in.at[pl.ds(q * 8, 8)]
+        pltpu.make_async_copy(part, part, back_sem.at[q]).wait()
         rows = []
         for d in range(8):
             rows.append(jnp.concatenate(decode(back_in[q * 8 + d, :, 0:128], back_in[q * 8 + d, :, 128:256]), axis=1))
@@ -420,15 +463,15 @@
         scratch_shapes=[
             pltpu.VMEM(tiled, F32), pltpu.VMEM(flat, BF16), pltpu.VMEM(flat, BF16), pltpu.VMEM((NR, NR), F32),
             pltpu.VMEM((NR, NR), BF16), pltpu.VMEM((NR, NR), BF16), pltpu.VMEM((NR, NR), BF16), pltpu.VMEM((NR, NR), BF16),
-            pltpu.VMEM((ROWS, LEV, NPH), F32), pltpu.VMEM((2, LEV, NPH), F32), pltpu.VMEM(tiled, I32), pltpu.VMEM((ROWS, LEV, NPH), F32),
+            pltpu.VMEM((ROWS, LEV, NPH), F32), pltpu.VMEM((2, LEV, 1024), I32), pltpu.VMEM((2, LEV, 1024), I32), pltpu.VMEM((2, LEV, NPH), F32), pltpu.VMEM(tiled, I32), pltpu.VMEM((ROWS, LEV, NPH), F32),
             pltpu.VMEM((LEV, 128), F32), pltpu.VMEM((LEV, 128), F32),
             pltpu.VMEM((COLS, LEV, CELLS), I32), pltpu.VMEM((COLS, LEV, CELLS), I32),
             pltpu.VMEM((COLS, LEV, 256), I32), pltpu.VMEM((COLS, LEV, 256), I32),
             pltpu.VMEM((COLS, LEV, 256), I32), pltpu.VMEM((COLS, LEV, 256), I32),
-            pltpu.VMEM((ROWS, 64, NR), F32), pltpu.VMEM((2, PHD, NR), F32),
+            pltpu.VMEM((ROWS, 64, NR), F32), pltpu.VMEM((2, 32, NR), I32), pltpu.VMEM((2, 32, NR), I32), pltpu.VMEM((2, PHD, NR), F32),
             pltpu.VMEM((2, ROWS, NR), F32), pltpu.VMEM((2, ROWS, NR), F32),
             pltpu.VMEM((CELLS, NR), I32), pltpu.VMEM((CELLS, NR), F32), pltpu.VMEM((NR, CELLS), F32), pltpu.VMEM(tiled, F32),
-            dma((5,)), dma((11,)), dma((2,)), dma, dma, dma, dma, dma, dma((2,)), dma((2,)),
+            dma((5,)), dma((11,)), dma((2,)), dma, dma, dma, dma, dma((GROUPS,)), dma((2,)), dma((2,)),
         ],
         compiler_params=pltpu.CompilerParams(
             collective_id=0, has_side_effects=True, vmem_limit_bytes=60 * 2**20),

time: 55.5 us -> 52.4 us (0.944)
  Pallas kernels: 53.6 us -> 50.4 us
    pallas_call x1, Pallas kernels: 53.6 us -> 50.4 us  [per_device(): pl.pallas_call(kernel, out_shape=jax.ShapeDtypeStruct(flat, F32), in_spec...]
where the time goes in v2:
time: 52.4 us; the launch traced here: 52.2 us
  Pallas kernels  50.4 us (96%)
  local copies, waits for them, and re-layouts  1.77 us (3%)
    pallas_call x1, Pallas kernels, per_device(): pl.pallas_call(kernel, out_shape=jax.ShapeDtypeStruct(flat, F32), in_spec...  50.4 us
    unnamed x1, local copies, waits for them, and re-layouts  1.77 us

profile of v2, /device:TPU:6, one launch (start us, length us, event | category | flops | bytes accessed | tf_op | source)
XLA Modules:
  0.0 52.2 jit_solution(8373988385430607691)
XLA Ops:
  0.0 50.4 %shard_map.64 = f32[64,1536]{1,0:T(8,128)} custom-call(s32[2,8]{1,0:T(2,128)} %bitcast.14, s32[2,8]{1,0:T(2,128)} %bitcast.15, f32[64,1536]{1,0:T(8,128)} %bitcast.11, bf16[64,1536]{1,0:T(8,128)(2,1)} %bitcast.12, bf16[64,1536]{1,0:T(8,128)(2,1)} %bitcast.13, f32[256,256]{1,0:T(8,128)} %mat_hbm.1), custom_call_target="tpu_custom_call" | custom-call | tf_op jit(solution)/shard_map/pallas_call | solution.py:458
  50.4 1.8 %copy.8 = f32[1,8,8,1536]{3,2,1,0:T(8,128)} copy(f32[1,8,8,1536]{3,2,1,0:T(8,128)} %bitcast.10) | data formatting | bytes 786432

commit v3 on v2

--- a/solution.py
+++ b/solution.py
@@ -19,6 +19,7 @@
 GROUPS = NPH // CELLS
 TILES = NPH // 128
 VEL_ONE = 32767.0
+ORDER = (1, 2, 3, 4, 5, 6, 0, 7)
 F32 = jnp.float32
 I32 = jnp.int32
 BF16 = jnp.bfloat16
@@ -77,6 +78,38 @@
     )
 
 
+def scale_code(top, bits):
+    top = jnp.maximum(jnp.max(top, axis=1, keepdims=True), 1e-30)
+    return jnp.ceil(jnp.log2(jnp.broadcast_to(top, (top.shape[0], 128))) * 4.0).astype(I32) + (1 - 4 * bits)
+
+
+def quarter_power(k):
+    return jnp.exp2(k.astype(F32) * 0.25)
+
+
+def encode_early(x0, x1):
+    k = scale_code(jnp.maximum(jnp.abs(x0), jnp.abs(x1)), 15)
+    inverse = quarter_power(-k)
+    return (to_int(x0 * inverse) & 0xFFFF) | (to_int(x1 * inverse) << 16), k
+
+
+def encode_late(x, early):
+    k = scale_code(jnp.abs(x), 19)
+    lane = lax.broadcasted_iota(I32, x.shape, 1)
+    return (to_int(x * quarter_power(-k)) << 12) | (jnp.where(lane < 64, early, k) & 0xFFF)
+
+
+def decode_tiles(early, late):
+    k = (late << 20) >> 20
+    scale_early = jnp.broadcast_to(quarter_power(k[:, 0:1]), late.shape)
+    scale_late = jnp.broadcast_to(quarter_power(k[:, 127:128]), late.shape)
+    return (
+        ((early << 16) >> 16).astype(F32) * scale_early,
+        (early >> 16).astype(F32) * scale_early,
+        (late >> 12).astype(F32) * scale_late,
+    )
+
+
 def halves(x):
     high = x.astype(BF16)
     return high, (x - high.astype(F32)).astype(BF16)
@@ -94,9 +127,11 @@
     out_ref,
     field, vt, vp, mat, mat_h, mat_l, tmat_h, tmat_l,
     state, row_out, row_in, halo, words, star, ghost_out, ghost_in,
-    vel_out, vel_in, pack_out, pack_in, back_out, back_in,
+    vel_out, vel_in, early_out, early_in, late_out, late_in,
+    back_early_out, back_early_in, back_late_out, back_late_in, scales,
     column, side_out, side_in, side, edge_out, edge_in, vel_col, star_col, solved, tiles,
-    load_sem, send_sem, row_sem, ghost_sem, vela_sem, velb_sem, pack_sem, back_sem, side_sem, edge_sem,
+    load_sem, send_sem, row_sem, ghost_sem, vela_sem, velb_sem, early_sem, late_sem,
+    back_early_sem, back_late_sem, side_sem, edge_sem,
 ):
     p = lax.axis_index("panel")
     g = lax.axis_index("grp")
@@ -147,6 +182,25 @@
             w0, w1 = encode(*(state[t, :, CELLS * q + 128 * k : CELLS * q + 128 * (k + 1)] for k in range(3)))
             row_out[i, :, 256 * q : 256 * q + 128] = w0
             row_out[i, :, 256 * q + 128 : 256 * (q + 1)] = w1
+
+    count = COLS + jnp.where(g > 0, 1, 0) + jnp.where(g < 7, 1, 0)
+    pl.semaphore_wait(barrier, count)
+
+    def row_copy(sem, target):
+        return pltpu.make_async_remote_copy(
+            src_ref=row_out.at[sem], dst_ref=row_in.at[sem], send_sem=send_sem.at[sem], recv_sem=row_sem.at[sem],
+            device_id={"grp": target}, device_id_type=MESH)
+
+    up = row_copy(0, g + 1)
+    down = row_copy(1, g - 1)
+
+    @pl.when(g < 7)
+    def _():
+        up.start()
+
+    @pl.when(g > 0)
+    def _():
+        down.start()
 
     lane = lax.broadcasted_iota(I32, (LEV, 128), 1)
     ghosts = jnp.zeros((LEV, 128), F32)
@@ -164,6 +218,11 @@
             ghosts = jnp.where(lane == 2 * t + s, value, ghosts)
     ghost_out[...] = ghosts
 
+    ghost_copy = pltpu.make_async_remote_copy(
+        src_ref=ghost_out, dst_ref=ghost_in, send_sem=send_sem.at[2], recv_sem=ghost_sem,
+        device_id={"panel": 1 - p}, device_id_type=MESH)
+    ghost_copy.start()
+
     loads[1].wait()
     loads[2].wait()
     for k in range(TILES):
@@ -171,7 +230,7 @@
 
     def vel_group(q, carry):
         rows = []
-        for t in range(ROWS):
+        for t in ORDER:
             parts = [words[q * 3 + k, pl.ds(t, LEV, stride=ROWS), :] for k in range(3)]
             rows.append(jnp.concatenate(parts, axis=1))
         for d, row in enumerate(swap_chunks(rows)):
@@ -179,30 +238,6 @@
         return carry
 
     lax.fori_loop(0, GROUPS, vel_group, 0)
-
-    count = COLS + jnp.where(g > 0, 1, 0) + jnp.where(g < 7, 1, 0)
-    pl.semaphore_wait(barrier, count)
-
-    def row_copy(sem, target):
-        return pltpu.make_async_remote_copy(
-            src_ref=row_out.at[sem], dst_ref=row_in.at[sem], send_sem=send_sem.at[sem], recv_sem=row_sem.at[sem],
-            device_id={"grp": target}, device_id_type=MESH)
-
-    up = row_copy(0, g + 1)
-    down = row_copy(1, g - 1)
-
-    @pl.when(g < 7)
-    def _():
-        up.start()
-
-    @pl.when(g > 0)
-    def _():
-        down.start()
-
-    ghost_copy = pltpu.make_async_remote_copy(
-        src_ref=ghost_out, dst_ref=ghost_in, send_sem=send_sem.at[2], recv_sem=ghost_sem,
-        device_id={"panel": 1 - p}, device_id_type=MESH)
-    ghost_copy.start()
 
     def scatter(src, dst, lanes, send, recv):
         def part(ref, i):
@@ -247,25 +282,11 @@
 
     ghost_copy.wait_recv()
 
-    def unpack_row(i):
-        for q in range(GROUPS):
-            parts = decode(row_in[i, :, 256 * q : 256 * q + 128], row_in[i, :, 256 * q + 128 : 256 * (q + 1)])
-            for k, part in enumerate(parts):
-                halo[i, :, CELLS * q + 128 * k : CELLS * q + 128 * (k + 1)] = part
-
-    @pl.when(g > 0)
-    def _():
-        up.wait_recv()
-        unpack_row(0)
-
-    @pl.when(g < 7)
-    def _():
-        down.wait_recv()
-        unpack_row(1)
-
     wide = lax.broadcasted_iota(I32, (LEV, NPH), 1)
     ghosts = ghost_in[...]
-    for t in range(ROWS):
+
+    def star_row(place):
+        t = ORDER[place]
         center = state[t]
         south = state[t - 1] if t > 0 else halo[0]
         north = state[t + 1] if t < ROWS - 1 else halo[1]
@@ -274,38 +295,71 @@
         word = jnp.concatenate(
             [words[k, pl.ds(t, LEV, stride=ROWS), :] for k in range(TILES)], axis=1)
         half_t, half_p = half_vel(word)
-        star[t] = (
+        star[place] = (
             center + KAPPA * (north + south + east + west - 4.0 * center)
             - half_t * (north - south) - half_p * (east - west)
         )
 
-    def star_group(i, carry):
+    for place in range(6):
+        star_row(place)
+
+    def early_group(i, carry):
         q = lax.rem(own_group + i, GROUPS)
         lanes = pl.ds(pl.multiple_of(q * CELLS, 128), CELLS)
-        rows = swap_chunks([star[t, :, lanes] for t in range(ROWS)])
+        rows = swap_chunks([star[place if place < 6 else 0, :, lanes] for place in range(ROWS)])
         for d, row in enumerate(rows):
-            w0, w1 = encode(row[:, 0:128], row[:, 128:256], row[:, 256:384])
-            pack_out[q * 8 + d, :, 0:128] = w0
-            pack_out[q * 8 + d, :, 128:256] = w1
-        scatter_group(pack_out, pack_in, q, send_sem.at[4], pack_sem)
-        return carry
-
-    lax.fori_loop(0, GROUPS, star_group, 0)
-    scatter(vel_out, vel_in, second_part, send_sem.at[5], velb_sem)
-
+            word, k = encode_early(row[:, 0:128], row[:, 128:256])
+            early_out[q * 8 + d] = word
+            scales[pl.ds(pl.multiple_of(q * 64 + 8 * d, 8), 8), :] = k
+        scatter_group(early_out, early_in, q, send_sem.at[4], early_sem)
+        return carry
+
+    lax.fori_loop(0, GROUPS, early_group, 0)
+
+    def unpack_row(i):
+        for q in range(GROUPS):
+            parts = decode(row_in[i, :, 256 * q : 256 * q + 128], row_in[i, :, 256 * q + 128 : 256 * (q + 1)])
+            for k, part in enumerate(parts):
+                halo[i, :, CELLS * q + 128 * k : CELLS * q + 128 * (k + 1)] = part
+
+    @pl.when(g > 0)
+    def _():
+        up.wait_recv()
+        unpack_row(0)
+
+    @pl.when(g < 7)
+    def _():
+        down.wait_recv()
+        unpack_row(1)
+
+    star_row(6)
+    star_row(7)
+
+    def late_group(i, carry):
+        q = lax.rem(own_group + i, GROUPS)
+        lanes = pl.ds(pl.multiple_of(q * CELLS, 128), CELLS)
+        rows = swap_chunks([star[place, :, lanes] for place in range(ROWS)])
+        for d, row in enumerate(rows):
+            k = scales[pl.ds(pl.multiple_of(q * 64 + 8 * d, 8), 8), :]
+            late_out[q * 8 + d] = encode_late(row[:, 256:384], k)
+        scatter_group(late_out, late_in, q, send_sem.at[11], late_sem)
+        return carry
+
+    lax.fori_loop(0, GROUPS, late_group, 0)
     loads[3].wait()
     matrix = mat[...]
     mat_h[...], mat_l[...] = halves(matrix)
     tmat_h[...], tmat_l[...] = halves(jnp.transpose(matrix))
 
-    arrived(pack_in, None, pack_sem)
-    w0 = pack_in[:, :, 0:128].reshape(NR, 128)
-    w1 = pack_in[:, :, 128:256].reshape(NR, 128)
-    for i, tile in enumerate(decode(w0, w1)):
+    arrived(early_in, None, early_sem)
+    arrived(late_in, None, late_sem)
+    scatter(vel_out, vel_in, second_part, send_sem.at[5], velb_sem)
+    tiles1 = decode_tiles(early_in[...].reshape(NR, 128), late_in[...].reshape(NR, 128))
+    for i, tile in enumerate(tiles1):
         star_col[pl.ds(128 * i, 128), :] = jnp.transpose(tile)
     first = dot3(halves(star_col[...]), (tmat_h[...], tmat_l[...]), ((1,), (0,)))
-    for t in range(ROWS):
-        column[t, pl.ds(8, PHD), :] = first[t * PHD : (t + 1) * PHD]
+    for place, t in enumerate(ORDER):
+        column[t, pl.ds(8, PHD), :] = first[place * PHD : (place + 1) * PHD]
 
     @pl.when(g == 0)
     def _():
@@ -378,39 +432,58 @@
         column[t, pl.ds(7, 1), :] = edge_in[0, pl.ds(t, 1), :]
         column[t, pl.ds(8 + PHD, 1), :] = edge_in[1, pl.ds(t, 1), :]
 
-    @pl.when(g > 0)
-    def _():
-        up2.wait_recv()
-        unpack_side(0)
-
-    @pl.when(g < 7)
-    def _():
-        down2.wait_recv()
-        unpack_side(1)
-
-    for t in range(ROWS):
+    def column_star(place):
+        t = ORDER[place]
         center = column[t, inner, :]
         south = column[t - 1, inner, :] if t > 0 else side[0]
         north = column[t + 1, inner, :] if t < ROWS - 1 else side[1]
         east = column[t, pl.ds(9, PHD), :]
         west = column[t, pl.ds(7, PHD), :]
-        half_t, half_p = half_vel(vel_col[pl.ds(t * PHD, PHD), :])
-        star_col[pl.ds(t * PHD, PHD), :] = (
+        half_t, half_p = half_vel(vel_col[pl.ds(place * PHD, PHD), :])
+        star_col[pl.ds(place * PHD, PHD), :] = (
             center + KAPPA * (north + south + east + west - 4.0 * center)
             - half_t * (north - south) - half_p * (east - west)
         )
-    solved[...] = dot3((mat_h[...], mat_l[...]), halves(star_col[...]), ((1,), (1,)))
-
-    def back_group(i, carry):
+
+    matrix_halves = mat_h[...], mat_l[...]
+    for place in range(6):
+        column_star(place)
+    solved[:, 0:256] = dot3(matrix_halves, halves(star_col[0:256]), ((1,), (1,)))
+
+    def back_early_group(i, carry):
         q = lax.rem(own_group + i, GROUPS)
         rows = pl.ds(pl.multiple_of(q * 64, 64), 64)
-        w0, w1 = encode(solved[rows, 0:128], solved[rows, 128:256], solved[rows, 256:384])
-        back_out[pl.ds(q * 8, 8), :, 0:128] = w0.reshape(8, LEV, 128)
-        back_out[pl.ds(q * 8, 8), :, 128:256] = w1.reshape(8, LEV, 128)
-        scatter_group(back_out, back_in, q, send_sem.at[10], back_sem.at[own_group])
-        return carry
-
-    lax.fori_loop(0, GROUPS, back_group, 0)
+        word, k = encode_early(solved[rows, 0:128], solved[rows, 128:256])
+        back_early_out[pl.ds(q * 8, 8)] = word.reshape(8, LEV, 128)
+        scales[rows, :] = k
+        scatter_group(back_early_out, back_early_in, q, send_sem.at[10], back_early_sem.at[own_group])
+        return carry
+
+    lax.fori_loop(0, GROUPS, back_early_group, 0)
+
+    @pl.when(g > 0)
+    def _():
+        up2.wait_recv()
+        unpack_side(0)
+
+    @pl.when(g < 7)
+    def _():
+        down2.wait_recv()
+        unpack_side(1)
+
+    column_star(6)
+    column_star(7)
+    solved[:, 256:384] = dot3(matrix_halves, halves(star_col[256:384]), ((1,), (1,)))
+
+    def back_late_group(i, carry):
+        q = lax.rem(own_group + i, GROUPS)
+        rows = pl.ds(pl.multiple_of(q * 64, 64), 64)
+        word = encode_late(solved[rows, 256:384], scales[rows, :])
+        back_late_out[pl.ds(q * 8, 8)] = word.reshape(8, LEV, 128)
+        scatter_group(back_late_out, back_late_in, q, send_sem.at[12], back_late_sem.at[own_group])
+        return carry
+
+    lax.fori_loop(0, GROUPS, back_late_group, 0)
 
     @pl.when(g < 7)
     def _():
@@ -426,17 +499,19 @@
     for copy in edge_copies:
         copy.wait_send()
     sent(vel_out, first_part, send_sem.at[3])
-    sent(pack_out, None, send_sem.at[4])
+    sent(early_out, None, send_sem.at[4])
+    sent(late_out, None, send_sem.at[11])
     sent(vel_out, second_part, send_sem.at[5])
 
     def out_group(i, carry):
         q = lax.rem(own_group + GROUPS - i, GROUPS)
-        part = back_in.at[pl.ds(q * 8, 8)]
-        pltpu.make_async_copy(part, part, back_sem.at[q]).wait()
+        for part, sem in ((back_early_in, back_early_sem), (back_late_in, back_late_sem)):
+            part = part.at[pl.ds(q * 8, 8)]
+            pltpu.make_async_copy(part, part, sem.at[q]).wait()
         rows = []
         for d in range(8):
-            rows.append(jnp.concatenate(decode(back_in[q * 8 + d, :, 0:128], back_in[q * 8 + d, :, 128:256]), axis=1))
-        for t, row in enumerate(swap_chunks(rows)):
+            rows.append(jnp.concatenate(decode_tiles(back_early_in[q * 8 + d], back_late_in[q * 8 + d]), axis=1))
+        for t, row in zip(ORDER, swap_chunks(rows)):
             for k in range(3):
                 tiles[q * 3 + k, pl.ds(t, LEV, stride=ROWS), :] = row[:, 128 * k : 128 * (k + 1)]
         for k in range(3):
@@ -446,7 +521,8 @@
 
     lax.fori_loop(0, GROUPS, out_group, 0)
     pltpu.make_async_copy(tiles, tiles, load_sem.at[4]).wait()
-    sent(back_out, None, send_sem.at[10])
+    sent(back_early_out, None, send_sem.at[10])
+    sent(back_late_out, None, send_sem.at[12])
 
 
 def per_device(field, vel_theta, vel_phi, strip_cell, strip_dir, radial_inverse):
@@ -466,12 +542,12 @@
             pltpu.VMEM((ROWS, LEV, NPH), F32), pltpu.VMEM((2, LEV, 1024), I32), pltpu.VMEM((2, LEV, 1024), I32), pltpu.VMEM((2, LEV, NPH), F32), pltpu.VMEM(tiled, I32), pltpu.VMEM((ROWS, LEV, NPH), F32),
             pltpu.VMEM((LEV, 128), F32), pltpu.VMEM((LEV, 128), F32),
             pltpu.VMEM((COLS, LEV, CELLS), I32), pltpu.VMEM((COLS, LEV, CELLS), I32),
-            pltpu.VMEM((COLS, LEV, 256), I32), pltpu.VMEM((COLS, LEV, 256), I32),
-            pltpu.VMEM((COLS, LEV, 256), I32), pltpu.VMEM((COLS, LEV, 256), I32),
+            *[pltpu.VMEM((COLS, LEV, 128), I32)] * 8, pltpu.VMEM((NR, 128), I32),
             pltpu.VMEM((ROWS, 64, NR), F32), pltpu.VMEM((2, 32, NR), I32), pltpu.VMEM((2, 32, NR), I32), pltpu.VMEM((2, PHD, NR), F32),
             pltpu.VMEM((2, ROWS, NR), F32), pltpu.VMEM((2, ROWS, NR), F32),
             pltpu.VMEM((CELLS, NR), I32), pltpu.VMEM((CELLS, NR), F32), pltpu.VMEM((NR, CELLS), F32), pltpu.VMEM(tiled, F32),
-            dma((5,)), dma((11,)), dma((2,)), dma, dma, dma, dma, dma((GROUPS,)), dma((2,)), dma((2,)),
+            dma((5,)), dma((13,)), dma((2,)), dma, dma, dma, dma, dma,
+            dma((GROUPS,)), dma((GROUPS,)), dma((2,)), dma((2,)),
         ],
         compiler_params=pltpu.CompilerParams(
             collective_id=0, has_side_effects=True, vmem_limit_bytes=60 * 2**20),

time: 52.4 us -> 49.5 us (0.945)
  Pallas kernels: 50.4 us -> 47.5 us
    pallas_call x1, Pallas kernels: 50.4 us -> 47.5 us  [per_device(): pl.pallas_call(kernel, out_shape=jax.ShapeDtypeStruct(flat, F32), in_spec...]
where the time goes in v3:
time: 49.5 us; the launch traced here: 49.3 us
  Pallas kernels  47.5 us (96%)
  local copies, waits for them, and re-layouts  1.77 us (4%)
    pallas_call x1, Pallas kernels, per_device(): pl.pallas_call(kernel, out_shape=jax.ShapeDtypeStruct(flat, F32), in_spec...  47.5 us
    unnamed x1, local copies, waits for them, and re-layouts  1.77 us

profile of v3, /device:TPU:6, one launch (start us, length us, event | category | flops | bytes accessed | tf_op | source)
XLA Modules:
  0.0 49.3 jit_solution(5873483261217934643)
XLA Ops:
  0.0 47.5 %shard_map.64 = f32[64,1536]{1,0:T(8,128)} custom-call(s32[2,8]{1,0:T(2,128)} %bitcast.14, s32[2,8]{1,0:T(2,128)} %bitcast.15, f32[64,1536]{1,0:T(8,128)} %bitcast.11, bf16[64,1536]{1,0:T(8,128)(2,1)} %bitcast.12, bf16[64,1536]{1,0:T(8,128)(2,1)} %bitcast.13, f32[256,256]{1,0:T(8,128)} %mat_hbm.1), custom_call_target="tpu_custom_call" | custom-call | tf_op jit(solution)/shard_map/pallas_call | solution.py:534
  47.5 1.8 %copy.8 = f32[1,8,8,1536]{3,2,1,0:T(8,128)} copy(f32[1,8,8,1536]{3,2,1,0:T(8,128)} %bitcast.10) | data formatting | bytes 786432

commit v4 on v3

--- a/solution.py
+++ b/solution.py
@@ -130,7 +130,7 @@
     vel_out, vel_in, early_out, early_in, late_out, late_in,
     back_early_out, back_early_in, back_late_out, back_late_in, scales,
     column, side_out, side_in, side, edge_out, edge_in, vel_col, star_col, solved, tiles,
-    load_sem, send_sem, row_sem, ghost_sem, vela_sem, velb_sem, early_sem, late_sem,
+    load_sem, send_sem, row_sem, ghost_sem, vela_sem, velb_sem, velc_sem, early_sem, late_sem,
     back_early_sem, back_late_sem, side_sem, edge_sem,
 ):
     p = lax.axis_index("panel")
@@ -277,7 +277,7 @@
         most = src.at[pl.ds(0, COLS - 1)] if lanes is None else src.at[pl.ds(0, COLS - 1), :, lanes]
         pltpu.make_async_copy(most, most, send).wait()
 
-    first_part, second_part = pl.ds(0, 128), pl.ds(128, 256)
+    first_part, second_part, third_part = (pl.ds(128 * i, 128) for i in range(3))
     scatter(vel_out, vel_in, first_part, send_sem.at[3], vela_sem)
 
     ghost_copy.wait_recv()
@@ -351,9 +351,12 @@
     mat_h[...], mat_l[...] = halves(matrix)
     tmat_h[...], tmat_l[...] = halves(jnp.transpose(matrix))
 
+    sent(early_out, None, send_sem.at[4])
+    sent(late_out, None, send_sem.at[11])
+    scatter(vel_out, vel_in, second_part, send_sem.at[5], velb_sem)
     arrived(early_in, None, early_sem)
     arrived(late_in, None, late_sem)
-    scatter(vel_out, vel_in, second_part, send_sem.at[5], velb_sem)
+    scatter(vel_out, vel_in, third_part, send_sem.at[13], velc_sem)
     tiles1 = decode_tiles(early_in[...].reshape(NR, 128), late_in[...].reshape(NR, 128))
     for i, tile in enumerate(tiles1):
         star_col[pl.ds(128 * i, 128), :] = jnp.transpose(tile)
@@ -421,10 +424,13 @@
         for k, part in enumerate(decode(side_in[i, 0:16, :], side_in[i, 16:32, :])):
             side[i, 16 * k : 16 * (k + 1), :] = part
 
+    def turn(i):
+        vel_col[pl.ds(128 * i, 128), :] = jnp.transpose(vel_in[:, :, 128 * i : 128 * (i + 1)].reshape(NR, 128))
+
     arrived(vel_in, first_part, vela_sem)
     arrived(vel_in, second_part, velb_sem)
-    for i in range(3):
-        vel_col[pl.ds(128 * i, 128), :] = jnp.transpose(vel_in[:, :, 128 * i : 128 * (i + 1)].reshape(NR, 128))
+    turn(0)
+    turn(1)
 
     for s in range(2):
         pltpu.make_async_copy(edge_in.at[s], edge_in.at[s], edge_sem.at[s]).wait()
@@ -432,22 +438,24 @@
         column[t, pl.ds(7, 1), :] = edge_in[0, pl.ds(t, 1), :]
         column[t, pl.ds(8 + PHD, 1), :] = edge_in[1, pl.ds(t, 1), :]
 
-    def column_star(place):
+    def column_star(place, start=0, size=PHD):
         t = ORDER[place]
-        center = column[t, inner, :]
-        south = column[t - 1, inner, :] if t > 0 else side[0]
-        north = column[t + 1, inner, :] if t < ROWS - 1 else side[1]
-        east = column[t, pl.ds(9, PHD), :]
-        west = column[t, pl.ds(7, PHD), :]
-        half_t, half_p = half_vel(vel_col[pl.ds(place * PHD, PHD), :])
-        star_col[pl.ds(place * PHD, PHD), :] = (
+        part = pl.ds(8 + start, size)
+        center = column[t, part, :]
+        south = column[t - 1, part, :] if t > 0 else side[0]
+        north = column[t + 1, part, :] if t < ROWS - 1 else side[1]
+        east = column[t, pl.ds(9 + start, size), :]
+        west = column[t, pl.ds(7 + start, size), :]
+        half_t, half_p = half_vel(vel_col[pl.ds(place * PHD + start, size), :])
+        star_col[pl.ds(place * PHD + start, size), :] = (
             center + KAPPA * (north + south + east + west - 4.0 * center)
             - half_t * (north - south) - half_p * (east - west)
         )
 
     matrix_halves = mat_h[...], mat_l[...]
-    for place in range(6):
+    for place in range(5):
         column_star(place)
+    column_star(5, 0, 16)
     solved[:, 0:256] = dot3(matrix_halves, halves(star_col[0:256]), ((1,), (1,)))
 
     def back_early_group(i, carry):
@@ -461,6 +469,10 @@
 
     lax.fori_loop(0, GROUPS, back_early_group, 0)
 
+    arrived(vel_in, third_part, velc_sem)
+    turn(2)
+    column_star(5, 16, 32)
+
     @pl.when(g > 0)
     def _():
         up2.wait_recv()
@@ -499,9 +511,8 @@
     for copy in edge_copies:
         copy.wait_send()
     sent(vel_out, first_part, send_sem.at[3])
-    sent(early_out, None, send_sem.at[4])
-    sent(late_out, None, send_sem.at[11])
     sent(vel_out, second_part, send_sem.at[5])
+    sent(vel_out, third_part, send_sem.at[13])
 
     def out_group(i, carry):
         q = lax.rem(own_group + GROUPS - i, GROUPS)
@@ -535,7 +546,7 @@
         kernel,
         out_shape=jax.ShapeDtypeStruct(flat, F32),
         in_specs=[smem, smem, hbm, hbm, hbm, hbm],
-        out_specs=pl.BlockSpec(memory_space=pltpu.VMEM),
+        out_specs=pl.BlockSpec(memory_space=pl.ANY),
         scratch_shapes=[
             pltpu.VMEM(tiled, F32), pltpu.VMEM(flat, BF16), pltpu.VMEM(flat, BF16), pltpu.VMEM((NR, NR), F32),
             pltpu.VMEM((NR, NR), BF16), pltpu.VMEM((NR, NR), BF16), pltpu.VMEM((NR, NR), BF16), pltpu.VMEM((NR, NR), BF16),
@@ -546,7 +557,7 @@
             pltpu.VMEM((ROWS, 64, NR), F32), pltpu.VMEM((2, 32, NR), I32), pltpu.VMEM((2, 32, NR), I32), pltpu.VMEM((2, PHD, NR), F32),
             pltpu.VMEM((2, ROWS, NR), F32), pltpu.VMEM((2, ROWS, NR), F32),
             pltpu.VMEM((CELLS, NR), I32), pltpu.VMEM((CELLS, NR), F32), pltpu.VMEM((NR, CELLS), F32), pltpu.VMEM(tiled, F32),
-            dma((5,)), dma((13,)), dma((2,)), dma, dma, dma, dma, dma,
+            dma((5,)), dma((14,)), dma((2,)), dma, dma, dma, dma, dma, dma,
             dma((GROUPS,)), dma((GROUPS,)), dma((2,)), dma((2,)),
         ],
         compiler_params=pltpu.CompilerParams(

time: 49.5 us -> 47.7 us (0.964)
  Pallas kernels: 47.5 us -> 45.4 us
    pallas_call x1, Pallas kernels: 47.5 us -> 45.4 us  [per_device(): pl.pallas_call(kernel, out_shape=jax.ShapeDtypeStruct(flat, F32), in_spec...]
where the time goes in v4:
time: 47.7 us; the launch traced here: 47.2 us
  Pallas kernels  45.4 us (95%)
  local copies, waits for them, and re-layouts  1.77 us (4%)
    pallas_call x1, Pallas kernels, per_device(): pl.pallas_call(kernel, out_shape=jax.ShapeDtypeStruct(flat, F32), in_spec...  45.4 us
    unnamed x1, local copies, waits for them, and re-layouts  1.77 us

profile of v4, /device:TPU:6, one launch (start us, length us, event | category | flops | bytes accessed | tf_op | source)
XLA Modules:
  0.0 47.2 jit_solution(17316724761720677440)
XLA Ops:
  0.0 45.4 %shard_map.64 = f32[64,1536]{1,0:T(8,128)} custom-call(s32[2,8]{1,0:T(2,128)} %bitcast.14, s32[2,8]{1,0:T(2,128)} %bitcast.15, f32[64,1536]{1,0:T(8,128)} %bitcast.11, bf16[64,1536]{1,0:T(8,128)(2,1)} %bitcast.12, bf16[64,1536]{1,0:T(8,128)(2,1)} %bitcast.13, f32[256,256]{1,0:T(8,128)} %mat_hbm.1), custom_call_target="tpu_custom_call" | custom-call | tf_op jit(solution)/shard_map/pallas_call | solution.py:545
  45.4 1.8 %copy.8 = f32[1,8,8,1536]{3,2,1,0:T(8,128)} copy(f32[1,8,8,1536]{3,2,1,0:T(8,128)} %bitcast.10) | data formatting | bytes 786432

commit v5 on v4

--- a/solution.py
+++ b/solution.py
@@ -128,10 +128,10 @@
     field, vt, vp, mat, mat_h, mat_l, tmat_h, tmat_l,
     state, row_out, row_in, halo, words, star, ghost_out, ghost_in,
     vel_out, vel_in, early_out, early_in, late_out, late_in,
-    back_early_out, back_early_in, back_late_out, back_late_in, scales,
+    back_out, back_in, scales,
     column, side_out, side_in, side, edge_out, edge_in, vel_col, star_col, solved, tiles,
     load_sem, send_sem, row_sem, ghost_sem, vela_sem, velb_sem, velc_sem, early_sem, late_sem,
-    back_early_sem, back_late_sem, side_sem, edge_sem,
+    back_sem, side_sem, edge_sem,
 ):
     p = lax.axis_index("panel")
     g = lax.axis_index("grp")
@@ -458,44 +458,35 @@
     column_star(5, 0, 16)
     solved[:, 0:256] = dot3(matrix_halves, halves(star_col[0:256]), ((1,), (1,)))
 
-    def back_early_group(i, carry):
+    arrived(vel_in, third_part, velc_sem)
+    turn(2)
+    column_star(5, 16, 32)
+
+    @pl.when(g > 0)
+    def _():
+        up2.wait_recv()
+        unpack_side(0)
+
+    @pl.when(g < 7)
+    def _():
+        down2.wait_recv()
+        unpack_side(1)
+
+    column_star(6)
+    column_star(7)
+    solved[:, 256:384] = dot3(matrix_halves, halves(star_col[256:384]), ((1,), (1,)))
+
+    def back_group(i, carry):
         q = lax.rem(own_group + i, GROUPS)
         rows = pl.ds(pl.multiple_of(q * 64, 64), 64)
         word, k = encode_early(solved[rows, 0:128], solved[rows, 128:256])
-        back_early_out[pl.ds(q * 8, 8)] = word.reshape(8, LEV, 128)
-        scales[rows, :] = k
-        scatter_group(back_early_out, back_early_in, q, send_sem.at[10], back_early_sem.at[own_group])
+        late = encode_late(solved[rows, 256:384], k)
+        back_out[pl.ds(q * 8, 8), :, 0:128] = word.reshape(8, LEV, 128)
+        back_out[pl.ds(q * 8, 8), :, 128:256] = late.reshape(8, LEV, 128)
+        scatter_group(back_out, back_in, q, send_sem.at[10], back_sem.at[own_group])
         return carry
 
-    lax.fori_loop(0, GROUPS, back_early_group, 0)
-
-    arrived(vel_in, third_part, velc_sem)
-    turn(2)
-    column_star(5, 16, 32)
-
-    @pl.when(g > 0)
-    def _():
-        up2.wait_recv()
-        unpack_side(0)
-
-    @pl.when(g < 7)
-    def _():
-        down2.wait_recv()
-        unpack_side(1)
-
-    column_star(6)
-    column_star(7)
-    solved[:, 256:384] = dot3(matrix_halves, halves(star_col[256:384]), ((1,), (1,)))
-
-    def back_late_group(i, carry):
-        q = lax.rem(own_group + i, GROUPS)
-        rows = pl.ds(pl.multiple_of(q * 64, 64), 64)
-        word = encode_late(solved[rows, 256:384], scales[rows, :])
-        back_late_out[pl.ds(q * 8, 8)] = word.reshape(8, LEV, 128)
-        scatter_group(back_late_out, back_late_in, q, send_sem.at[12], back_late_sem.at[own_group])
-        return carry
-
-    lax.fori_loop(0, GROUPS, back_late_group, 0)
+    lax.fori_loop(0, GROUPS, back_group, 0)
 
     @pl.when(g < 7)
     def _():
@@ -516,12 +507,11 @@
 
     def out_group(i, carry):
         q = lax.rem(own_group + GROUPS - i, GROUPS)
-        for part, sem in ((back_early_in, back_early_sem), (back_late_in, back_late_sem)):
-            part = part.at[pl.ds(q * 8, 8)]
-            pltpu.make_async_copy(part, part, sem.at[q]).wait()
+        part = back_in.at[pl.ds(q * 8, 8)]
+        pltpu.make_async_copy(part, part, back_sem.at[q]).wait()
         rows = []
         for d in range(8):
-            rows.append(jnp.concatenate(decode_tiles(back_early_in[q * 8 + d], back_late_in[q * 8 + d]), axis=1))
+            rows.append(jnp.concatenate(decode_tiles(back_in[q * 8 + d, :, 0:128], back_in[q * 8 + d, :, 128:256]), axis=1))
         for t, row in zip(ORDER, swap_chunks(rows)):
             for k in range(3):
                 tiles[q * 3 + k, pl.ds(t, LEV, stride=ROWS), :] = row[:, 128 * k : 128 * (k + 1)]
@@ -532,8 +522,7 @@
 
     lax.fori_loop(0, GROUPS, out_group, 0)
     pltpu.make_async_copy(tiles, tiles, load_sem.at[4]).wait()
-    sent(back_early_out, None, send_sem.at[10])
-    sent(back_late_out, None, send_sem.at[12])
+    sent(back_out, None, send_sem.at[10])
 
 
 def per_device(field, vel_theta, vel_phi, strip_cell, strip_dir, radial_inverse):
@@ -553,12 +542,12 @@
             pltpu.VMEM((ROWS, LEV, NPH), F32), pltpu.VMEM((2, LEV, 1024), I32), pltpu.VMEM((2, LEV, 1024), I32), pltpu.VMEM((2, LEV, NPH), F32), pltpu.VMEM(tiled, I32), pltpu.VMEM((ROWS, LEV, NPH), F32),
             pltpu.VMEM((LEV, 128), F32), pltpu.VMEM((LEV, 128), F32),
             pltpu.VMEM((COLS, LEV, CELLS), I32), pltpu.VMEM((COLS, LEV, CELLS), I32),
-            *[pltpu.VMEM((COLS, LEV, 128), I32)] * 8, pltpu.VMEM((NR, 128), I32),
+            *[pltpu.VMEM((COLS, LEV, 128), I32)] * 4, *[pltpu.VMEM((COLS, LEV, 256), I32)] * 2, pltpu.VMEM((NR, 128), I32),
             pltpu.VMEM((ROWS, 64, NR), F32), pltpu.VMEM((2, 32, NR), I32), pltpu.VMEM((2, 32, NR), I32), pltpu.VMEM((2, PHD, NR), F32),
             pltpu.VMEM((2, ROWS, NR), F32), pltpu.VMEM((2, ROWS, NR), F32),
             pltpu.VMEM((CELLS, NR), I32), pltpu.VMEM((CELLS, NR), F32), pltpu.VMEM((NR, CELLS), F32), pltpu.VMEM(tiled, F32),
             dma((5,)), dma((14,)), dma((2,)), dma, dma, dma, dma, dma, dma,
-            dma((GROUPS,)), dma((GROUPS,)), dma((2,)), dma((2,)),
+            dma((GROUPS,)), dma((2,)), dma((2,)),
         ],
         compiler_params=pltpu.CompilerParams(
             collective_id=0, has_side_effects=True, vmem_limit_bytes=60 * 2**20),

time: 47.7 us -> 48 us (level)
  Pallas kernels: 45.4 us -> 46 us
    pallas_call x1, Pallas kernels: 45.4 us -> 46 us  [per_device(): pl.pallas_call(kernel, out_shape=jax.ShapeDtypeStruct(flat, F32), in_spec...]
where the time goes in v5:
time: 48 us; the launch traced here: 47.8 us
  Pallas kernels  46 us (96%)
  local copies, waits for them, and re-layouts  1.77 us (4%)
    pallas_call x1, Pallas kernels, per_device(): pl.pallas_call(kernel, out_shape=jax.ShapeDtypeStruct(flat, F32), in_spec...  46 us
    unnamed x1, local copies, waits for them, and re-layouts  1.77 us

profile of v5, /device:TPU:6, one launch (start us, length us, event | category | flops | bytes accessed | tf_op | source)
XLA Modules:
  0.0 47.8 jit_solution(10879014218383951063)
XLA Ops:
  0.0 46.0 %shard_map.64 = f32[64,1536]{1,0:T(8,128)} custom-call(s32[2,8]{1,0:T(2,128)} %bitcast.14, s32[2,8]{1,0:T(2,128)} %bitcast.15, f32[64,1536]{1,0:T(8,128)} %bitcast.11, bf16[64,1536]{1,0:T(8,128)(2,1)} %bitcast.12, bf16[64,1536]{1,0:T(8,128)(2,1)} %bitcast.13, f32[256,256]{1,0:T(8,128)} %mat_hbm.1), custom_call_target="tpu_custom_call" | custom-call | tf_op jit(solution)/shard_map/pallas_call | solution.py:534
  46.0 1.8 %copy.8 = f32[1,8,8,1536]{3,2,1,0:T(8,128)} copy(f32[1,8,8,1536]{3,2,1,0:T(8,128)} %bitcast.10) | data formatting | bytes 786432

commit v6 on v5

--- a/solution.py
+++ b/solution.py
@@ -356,7 +356,6 @@
     scatter(vel_out, vel_in, second_part, send_sem.at[5], velb_sem)
     arrived(early_in, None, early_sem)
     arrived(late_in, None, late_sem)
-    scatter(vel_out, vel_in, third_part, send_sem.at[13], velc_sem)
     tiles1 = decode_tiles(early_in[...].reshape(NR, 128), late_in[...].reshape(NR, 128))
     for i, tile in enumerate(tiles1):
         star_col[pl.ds(128 * i, 128), :] = jnp.transpose(tile)
@@ -419,6 +418,8 @@
             device_id={"panel": panel, "col": there}, device_id_type=MESH)
         copy.start()
         edge_copies.append(copy)
+
+    scatter(vel_out, vel_in, third_part, send_sem.at[13], velc_sem)
 
     def unpack_side(i):
         for k, part in enumerate(decode(side_in[i, 0:16, :], side_in[i, 16:32, :])):

time: 48 us -> 48.7 us (1.015)
  Pallas kernels: 46 us -> 46.8 us
    pallas_call x1, Pallas kernels: 46 us -> 46.8 us  [per_device(): pl.pallas_call(kernel, out_shape=jax.ShapeDtypeStruct(flat, F32), in_spec...]
where the time goes in v6:
time: 48.7 us; the launch traced here: 48.5 us
  Pallas kernels  46.8 us (96%)
  local copies, waits for them, and re-layouts  1.77 us (4%)
    pallas_call x1, Pallas kernels, per_device(): pl.pallas_call(kernel, out_shape=jax.ShapeDtypeStruct(flat, F32), in_spec...  46.8 us
    unnamed x1, local copies, waits for them, and re-layouts  1.77 us

profile of v6, /device:TPU:6, one launch (start us, length us, event | category | flops | bytes accessed | tf_op | source)
XLA Modules:
  0.0 48.5 jit_solution(3025850431206595599)
XLA Ops:
  0.0 46.8 %shard_map.64 = f32[64,1536]{1,0:T(8,128)} custom-call(s32[2,8]{1,0:T(2,128)} %bitcast.14, s32[2,8]{1,0:T(2,128)} %bitcast.15, f32[64,1536]{1,0:T(8,128)} %bitcast.11, bf16[64,1536]{1,0:T(8,128)(2,1)} %bitcast.12, bf16[64,1536]{1,0:T(8,128)(2,1)} %bitcast.13, f32[256,256]{1,0:T(8,128)} %mat_hbm.1), custom_call_target="tpu_custom_call" | custom-call | tf_op jit(solution)/shard_map/pallas_call | solution.py:535
  46.8 1.8 %copy.8 = f32[1,8,8,1536]{3,2,1,0:T(8,128)} copy(f32[1,8,8,1536]{3,2,1,0:T(8,128)} %bitcast.10) | data formatting | bytes 786432
